TPU v7x, 128 devices: a whole 4x4x4 slice. The times are simulated.
128 devices in a mesh: exp: 8 (over y, z_hi), gy: 4 (over z_lo, core), gz: 4 (over x).
Axes of the slice: x: 4, y: 4, z: 4 (z_hi: 2, z_lo: 2; z = z_hi * 2 + z_lo), core: 2. Of those that a mesh axis runs over, the one named last changes fastest.
Arguments:
- adjoint_final: float32 [8, 128, 128, 1024], P('exp', None, 'gy', 'gz'), may hold values from -6 to 6
- concentration: bfloat16 [2, 8, 128, 128, 1024], P(None, 'exp', None, 'gy', 'gz'), may hold values from 0 to 1
- observed: bfloat16 [2, 8, 128, 128, 1024], P(None, 'exp', None, 'gy', 'gz'), may hold values from 0 to 1
- capacity: float32 [128, 128, 1024], P(None, 'gy', 'gz'), may hold values from 0.03 to 0.3
- pore_mask: int32 [128, 128, 1024], P(None, 'gy', 'gz'), may hold values 0 or 1
- feed_index: int32 [8], P('exp'), may hold values from 0 to 7
- feed_affinity: float32 [8], replicated, may hold values from 0.5 to 4
Outputs:
- adjoint_first: float32 [8, 128, 128, 1024], P('exp', None, 'gy', 'gz')
- capacity_grad: float32 [128, 128, 1024], P('exp', 'gy', 'gz')
All inputs are finite; a program needn't handle non-finite values. No bound on the sum of `pore_mask` on one device may be relied on, other than what follows from the above.
Results may differ from a plain program's by a relative error of at most 0.0003.
Values sent between devices are 32-bit elements; how exact they have to be, the bound alone decides.
No kernel may reach another device: no remote copies, remote signals or barrier semaphores. Data moves between devices by JAX's collectives and lax.ppermute only.
A program may use at most 128 MiB of HBM per device.

v0:
```python
import jax
import jax.numpy as jnp
from jax import lax
from jax.sharding import PartitionSpec as P


def padded(cells, sides, width):
    for axis, dim in sides:
        count = lax.axis_size(axis)
        ends = count - 1
        head = lax.slice_in_dim(cells, 0, width, axis=dim)
        tail = lax.slice_in_dim(cells, cells.shape[dim] - width, cells.shape[dim], axis=dim)
        cells = jnp.concatenate(
            [
                lax.ppermute(tail, axis, [(i, (i + 1) % count) for i in range(ends)]),
                cells,
                lax.ppermute(head, axis, [((i + 1) % count, i) for i in range(ends)]),
            ],
            axis=dim,
        )
    return cells


def face_flux(near_adj, near_pores, adjoint):
    return near_pores * (near_adj - adjoint)


def adjoint_update(adjoint_wide, pores_wide, capacity, affinity, filled_low, observed_low):
    adjoint = adjoint_wide[:, 1:-1, 1:-1]
    pores = pores_wide[:, 1:-1, 1:-1]
    adjoint_x = jnp.pad(adjoint, ((1, 1), (0, 0), (0, 0)))
    pores_x = jnp.pad(pores, ((1, 1), (0, 0), (0, 0)))
    dispersion = face_flux(adjoint_x[2:], pores_x[2:], adjoint) + face_flux(
        adjoint_x[:-2], pores_x[:-2], adjoint
    )
    dispersion = dispersion + face_flux(adjoint_wide[:, 2:, 1:-1], pores_wide[:, 2:, 1:-1], adjoint)
    dispersion = dispersion + face_flux(
        adjoint_wide[:, :-2, 1:-1], pores_wide[:, :-2, 1:-1], adjoint
    )
    dispersion = dispersion + face_flux(adjoint_wide[:, 1:-1, 2:], pores_wide[:, 1:-1, 2:], adjoint)
    dispersion = dispersion + face_flux(
        adjoint_wide[:, 1:-1, :-2], pores_wide[:, 1:-1, :-2], adjoint
    )
    pores_next = jnp.concatenate([pores[1:], jnp.ones_like(pores[:1])], 0)
    adjoint_next = jnp.concatenate([adjoint[1:], jnp.zeros_like(adjoint[:1])], 0)
    transport = pores_next * (adjoint_next - adjoint)
    filled = filled_low.astype(jnp.float32)
    saturation = 1.0 + affinity * filled
    uptake = capacity * affinity / (saturation * saturation)
    updated = pores * (
        adjoint
        + 0.1 * dispersion
        + 0.2 * transport
        - uptake * adjoint
        + (filled - observed_low.astype(jnp.float32))
    )
    gradient_term = -pores * affinity * filled / saturation * adjoint
    return (updated, gradient_term)


def shards(adjoint_final, concentration, observed, capacity, pore_mask, feed_index, feed_affinity):
    pores_wide = padded(pore_mask, (("gy", 1), ("gz", 2)), 1).astype(jnp.float32)
    feeds = jnp.arange(feed_affinity.shape[0], dtype=jnp.int32)
    affinity = jnp.sum(
        jnp.where(feeds == feed_index[0], feed_affinity, jnp.zeros_like(feed_affinity))
    )
    adjoint = adjoint_final[0]
    length = adjoint.shape[0]
    share = length // lax.axis_size("exp")
    gradient = jnp.zeros_like(adjoint)
    for moment in reversed(range(concentration.shape[0])):
        adjoint_wide = padded(adjoint, (("gy", 1), ("gz", 2)), 1)
        adjoint, gradient_term = adjoint_update(
            adjoint_wide,
            pores_wide,
            capacity,
            affinity,
            concentration[moment, 0],
            observed[moment, 0],
        )
        gradient = gradient + gradient_term
    summed = lax.psum(gradient, "exp")
    owned = lax.dynamic_slice_in_dim(summed, lax.axis_index("exp") * share, share, 0)
    return (adjoint[None], owned)


def solution(mesh):
    in_specs = (
        P("exp", None, "gy", "gz"),
        P(None, "exp", None, "gy", "gz"),
        P(None, "exp", None, "gy", "gz"),
        P(None, "gy", "gz"),
        P(None, "gy", "gz"),
        P("exp"),
        P(),
    )
    out_specs = (P("exp", None, "gy", "gz"), P("exp", "gy", "gz"))
    return jax.shard_map(shards, mesh=mesh, in_specs=in_specs, out_specs=out_specs, check_vma=False)
```

profile of v0, /device:TPU:16, one launch (start us, length us, event | category | flops | bytes accessed | tf_op | source)
XLA Modules:
  0.0 328.1 jit_solution(10019507288806775459)
XLA Ops:
  12.0 6.0 %copy.14 = f32[1,128,32,256]{1,2,3,0:T(8,128)} copy(f32[1,128,32,256]{3,2,1,0:T(8,128)} %param.7) | data formatting | bytes 8388608 | tf_op args[0]
  21.3 5.6 %collective-permute-start.5 = (f32[128,1,256]{2,0,1:T(8,128)S(1)}, f32[128,1,256]{2,0,1:T(8,128)S(1)}, u32[]{:S(2)}, u32[]{:S(2)}) collective-permute-start(f32[128,1,256]{2,0,1:T(8,128)S(1)} %copy.17), channel_id=1, source_target_pairs={{0,4},{4,8},{8,12},{1,5},{5,9},{9,13},{2,6},{6,10},{10,14},{3,7},{... | collective-permute-start | bytes 393224 | tf_op jit(solution)/shard_map/ppermute | solution.py:15
  26.9 5.3 %slice_bitcast_fusion = f32[127,32,256]{0,1,2:T(8,128)} fusion(f32[1,128,32,256]{1,2,3,0:T(8,128)} %copy.14), kind=kLoop, calls=%fused_computation.72 | loop fusion | bytes 8323072 | tf_op jit(solution)/shard_map/slice | solution.py:45
  32.2 2.6 fusion.65
  39.0 5.9 %copy.12 = s32[128,32,256]{0,1,2:T(8,128)} copy(s32[128,32,256]{2,1,0:T(8,128)} %param.11) | data formatting | bytes 8388608 | tf_op args[4]
  44.9 5.2 %copy.39 = bf16[1,1,128,32,256]{2,3,4,1,0:T(8,128)(2,1)} copy(bf16[1,1,128,32,256]{4,3,2,1,0:T(8,128)(2,1)} %get-tuple-element.19) | data formatting | bytes 4194304
  50.0 5.2 %copy.37 = bf16[1,1,128,32,256]{2,3,4,1,0:T(8,128)(2,1)} copy(bf16[1,1,128,32,256]{4,3,2,1,0:T(8,128)(2,1)} %get-tuple-element.18) | data formatting | bytes 4194304
  55.2 4.0 %copy.38 = bf16[1,1,128,32,256]{2,3,4,1,0:T(8,128)(2,1)} copy(bf16[1,1,128,32,256]{4,3,2,1,0:T(8,128)(2,1)S(1)} %get-tuple-element.13) | data formatting | bytes 4194304
  59.3 6.0 %copy.22 = f32[128,32,256]{0,1,2:T(8,128)} copy(f32[128,32,256]{2,1,0:T(8,128)} %param.10) | data formatting | bytes 8388608 | tf_op args[3]
  66.2 3.4 %collective-permute-start.2 = (s32[128,34,1]{0,1,2:T(8,128)S(1)}, s32[128,34,1]{0,1,2:T(8,128)S(1)}, u32[]{:S(2)}, u32[]{:S(2)}) collective-permute-start(s32[128,34,1]{0,1,2:T(8,128)S(1)} %get-tuple-element.10), channel_id=1, source_target_pairs={{0,1},{1,2},{2,3},{4,5},{5,6},{6,7},{8,9},{9,10},{10,11},{12,13},{... | collective-permute-start | bytes 52232 | tf_op jit(solution)/shard_map/ppermute | solution.py:15
  73.4 5.4 %collective-permute-start.7 = (f32[128,34,1]{0,1,2:T(8,128)S(1)}, f32[128,34,1]{0,1,2:T(8,128)S(1)}, u32[]{:S(2)}, u32[]{:S(2)}) collective-permute-start(f32[128,34,1]{0,1,2:T(8,128)S(1)} %get-tuple-element.9), channel_id=1, source_target_pairs={{0,1},{1,2},{2,3},{4,5},{5,6},{6,7},{8,9},{9,10},{10,11},{12,13},{... | collective-permute-start | bytes 52232 | tf_op jit(solution)/shard_map/ppermute | solution.py:15
  78.8 1.9 add_convert_fusion
  80.7 3.1 slice.173
  83.8 3.2 slice.180
  87.1 32.2 %fusion.9 = (f32[128,32,256]{0,1,2:T(8,128)}, f32[128,32,256]{0,1,2:T(8,128)}) fusion(bf16[1,1,128,32,256]{2,3,4,1,0:T(8,128)(2,1)} %copy.39, bf16[1,1,128,32,256]{2,3,4,1,0:T(8,128)(2,1)} %copy.37, f32[]{:T(128)} %fusion.60, f32[1,128,32,256]{1,2,3,0:T(8,128)} %copy.14, f32[128,34,258]{0,1,2:T(8,128)S(1)} %add_convert_fusion, f32[128,32,256]{0,1,2:T(8,128)} %slice.173, ...), kind=kLoop, calls=%fused_computation.22 | loop fusion | flops 57671680 | bytes 61048836 | tf_op jit(solution)/shard_map/add | solution.py:81
  122.5 3.4 %collective-permute-start.9 = (f32[128,1,256]{2,0,1:T(8,128)S(1)}, f32[128,1,256]{2,0,1:T(8,128)S(1)}, u32[]{:S(2)}, u32[]{:S(2)}) collective-permute-start(f32[128,1,256]{2,0,1:T(8,128)S(1)} %copy.27), channel_id=1, source_target_pairs={{0,4},{4,8},{8,12},{1,5},{5,9},{9,13},{2,6},{6,10},{10,14},{3,7},{... | collective-permute-start | bytes 393224 | tf_op jit(solution)/shard_map/ppermute | solution.py:15
  129.1 4.8 %collective-permute-start.11 = (f32[128,34,1]{0,1,2:T(8,128)S(1)}, f32[128,34,1]{0,1,2:T(8,128)S(1)}, u32[]{:S(2)}, u32[]{:S(2)}) collective-permute-start(f32[128,34,1]{0,1,2:T(8,128)S(1)} %get-tuple-element.7), channel_id=1, source_target_pairs={{0,1},{1,2},{2,3},{4,5},{5,6},{6,7},{8,9},{9,10},{10,11},{12,13},{... | collective-permute-start | bytes 52232 | tf_op jit(solution)/shard_map/ppermute | solution.py:15
  133.8 5.3 %copy.40 = bf16[1,1,128,32,256]{2,3,4,1,0:T(8,128)(2,1)} copy(bf16[1,1,128,32,256]{4,3,2,1,0:T(8,128)(2,1)} %get-tuple-element.12) | data formatting | bytes 4194304
  139.2 5.6 %slice.184 = f32[127,32,256]{0,1,2:T(8,128)} slice(f32[128,32,256]{0,1,2:T(8,128)} %get-tuple-element.5), slice={[1:128], [0:32], [0:256]} | slice | bytes 8323072 | tf_op jit(solution)/shard_map/slice | solution.py:45
  144.8 18.8 %fusion.59 = f32[1,128,32,256]{1,2,3,0:T(8,128)} fusion(f32[128,32,256]{0,1,2:T(8,128)} %slice.173, f32[128,32,256]{0,1,2:T(8,128)S(1)} %copy-done.1, f32[127,32,256]{0,1,2:T(8,128)} %slice.184, f32[128,1,256]{0,1,2:T(1,128)S(1)} %copy.26, f32[128,1,256]{0,1,2:T(1,128)S(1)} %copy.28, f32[128,34,1]{0,1,2:T(8,128)S(1)} %collective-permute-done.11, ...), kind=kLoop, calls=%fused_computation.89 | loop fusion | flops 45088768 | bytes 46368772 | tf_op jit(solution)/shard_map/broadcast_in_dim | solution.py:84
  163.7 5.5 %copy.33 = f32[1,128,32,256]{3,2,1,0:T(8,128)} copy(f32[1,128,32,256]{1,2,3,0:T(8,128)} %fusion.59) | data formatting | bytes 8388608
  169.2 142.3 %all-reduce.8.cloned.1.call-done = f32[128,32,256]{0,1,2:T(8,128)} async-done(((f32[128,32,256]{0,1,2:T(8,128)}), f32[128,32,256]{0,1,2:T(8,128)}) %all-reduce.8.cloned.1.call-update) | async-done | bytes 4194320 | tf_op jit(solution)/shard_map/psum | solution.py:82
  311.5 5.3 %constant_dynamic-slice_fusion = f32[16,32,256]{0,1,2:T(8,128)} fusion(f32[128,32,256]{0,1,2:T(8,128)} %all-reduce.8.cloned.1.call-done, s32[]{:T(128)S(6)} %select_n.8), kind=kLoop, calls=%fused_computation.101 | loop fusion | bytes 1048580 | tf_op jit(solution)/shard_map/dynamic_slice | solution.py:83
  316.8 4.5 %copy.34 = f32[16,32,256]{2,1,0:T(8,128)} copy(f32[16,32,256]{0,1,2:T(8,128)} %constant_dynamic-slice_fusion) | data formatting | bytes 1048576
  (60 shorter events, 22.7 us)
Async XLA Ops:
  7.2 304.3 %all-reduce.8.cloned.1.call-start = ((), (), s32[]{:S(2)}) async-start(), calls=%async_computation | async-start | bytes 8388608 | tf_op jit(solution)/shard_map/psum | solution.py:82
  9.0 56.3 %collective-permute-start = (s32[128,1,256]{2,0,1:T(8,128)S(1)}, s32[128,1,256]{2,0,1:T(8,128)S(1)}, u32[]{:S(2)}, u32[]{:S(2)}) collective-permute-start(s32[128,1,256]{2,0,1:T(8,128)S(1)} %copy.35), channel_id=1, source_target_pairs={{0,4},{4,8},{8,12},{1,5},{5,9},{9,13},{2,6},{6,10},{10,14},{3,7},{... | collective-permute-start | bytes 393224 | tf_op jit(solution)/shard_map/ppermute | solution.py:15
  10.7 54.6 %collective-permute-start.1 = (s32[128,1,256]{2,0,1:T(8,128)S(1)}, s32[128,1,256]{2,0,1:T(8,128)S(1)}, u32[]{:S(2)}, u32[]{:S(2)}) collective-permute-start(s32[128,1,256]{2,0,1:T(8,128)S(1)} %copy.36), channel_id=1, source_target_pairs={{4,0},{8,4},{12,8},{5,1},{9,5},{13,9},{6,2},{10,6},{14,10},{7,3},{... | collective-permute-start | bytes 393224 | tf_op jit(solution)/shard_map/ppermute | solution.py:17
  19.9 51.0 %collective-permute-start.4 = (f32[128,1,256]{2,0,1:T(8,128)S(1)}, f32[128,1,256]{2,0,1:T(8,128)S(1)}, u32[]{:S(2)}, u32[]{:S(2)}) collective-permute-start(f32[128,1,256]{2,0,1:T(8,128)S(1)} %copy.15), channel_id=1, source_target_pairs={{4,0},{8,4},{12,8},{5,1},{9,5},{13,9},{6,2},{10,6},{14,10},{7,3},{... | collective-permute-start | bytes 393224 | tf_op jit(solution)/shard_map/ppermute | solution.py:17
  21.3 10.9 %copy-start.4 = (bf16[2,1,128,32,256]{4,3,2,1,0:T(8,128)(2,1)S(1)}, bf16[2,1,128,32,256]{4,3,2,1,0:T(8,128)(2,1)}, u32[]{:S(2)}) copy-start(bf16[2,1,128,32,256]{4,3,2,1,0:T(8,128)(2,1)} %param.8) | copy-start | bytes 12582916
  21.3 49.7 %collective-permute-start.5 = (f32[128,1,256]{2,0,1:T(8,128)S(1)}, f32[128,1,256]{2,0,1:T(8,128)S(1)}, u32[]{:S(2)}, u32[]{:S(2)}) collective-permute-start(f32[128,1,256]{2,0,1:T(8,128)S(1)} %copy.17), channel_id=1, source_target_pairs={{0,4},{4,8},{8,12},{1,5},{5,9},{9,13},{2,6},{6,10},{10,14},{3,7},{... | collective-permute-start | bytes 393224 | tf_op jit(solution)/shard_map/ppermute | solution.py:15
  32.2 3.7 %copy-start.5 = (bf16[2,1,128,32,256]{4,3,2,1,0:T(8,128)(2,1)S(1)}, bf16[2,1,128,32,256]{4,3,2,1,0:T(8,128)(2,1)}, u32[]{:S(2)}) copy-start(bf16[2,1,128,32,256]{4,3,2,1,0:T(8,128)(2,1)} %param.9) | copy-start | bytes 12582916
  35.9 2.4 copy-start.6
  66.2 12.6 %collective-permute-start.2 = (s32[128,34,1]{0,1,2:T(8,128)S(1)}, s32[128,34,1]{0,1,2:T(8,128)S(1)}, u32[]{:S(2)}, u32[]{:S(2)}) collective-permute-start(s32[128,34,1]{0,1,2:T(8,128)S(1)} %get-tuple-element.10), channel_id=1, source_target_pairs={{0,1},{1,2},{2,3},{4,5},{5,6},{6,7},{8,9},{9,10},{10,11},{12,13},{... | collective-permute-start | bytes 52232 | tf_op jit(solution)/shard_map/ppermute | solution.py:15
  69.6 9.2 %collective-permute-start.3 = (s32[128,34,1]{0,1,2:T(8,128)S(1)}, s32[128,34,1]{0,1,2:T(8,128)S(1)}, u32[]{:S(2)}, u32[]{:S(2)}) collective-permute-start(s32[128,34,1]{0,1,2:T(8,128)S(1)} %get-tuple-element.11), channel_id=1, source_target_pairs={{1,0},{2,1},{3,2},{5,4},{6,5},{7,6},{9,8},{10,9},{11,10},{13,12},{... | collective-permute-start | bytes 52232 | tf_op jit(solution)/shard_map/ppermute | solution.py:17
  71.1 7.7 %copy-start.2 = (s32[128,32,256]{0,1,2:T(8,128)S(1)}, s32[128,32,256]{0,1,2:T(8,128)}, u32[]{:S(2)}) copy-start(s32[128,32,256]{0,1,2:T(8,128)} %copy.12) | copy-start | bytes 12582916
  72.0 15.1 %collective-permute-start.6 = (f32[128,34,1]{0,1,2:T(8,128)S(1)}, f32[128,34,1]{0,1,2:T(8,128)S(1)}, u32[]{:S(2)}, u32[]{:S(2)}) collective-permute-start(f32[128,34,1]{0,1,2:T(8,128)S(1)} %get-tuple-element.8), channel_id=1, source_target_pairs={{1,0},{2,1},{3,2},{5,4},{6,5},{7,6},{9,8},{10,9},{11,10},{13,12},{... | collective-permute-start | bytes 52232 | tf_op jit(solution)/shard_map/ppermute | solution.py:17
  73.4 13.7 %collective-permute-start.7 = (f32[128,34,1]{0,1,2:T(8,128)S(1)}, f32[128,34,1]{0,1,2:T(8,128)S(1)}, u32[]{:S(2)}, u32[]{:S(2)}) collective-permute-start(f32[128,34,1]{0,1,2:T(8,128)S(1)} %get-tuple-element.9), channel_id=1, source_target_pairs={{0,1},{1,2},{2,3},{4,5},{5,6},{6,7},{8,9},{9,10},{10,11},{12,13},{... | collective-permute-start | bytes 52232 | tf_op jit(solution)/shard_map/ppermute | solution.py:15
  80.7 6.3 %copy-start = (f32[128,34,258]{0,1,2:T(8,128)}, f32[128,34,258]{0,1,2:T(8,128)S(1)}, u32[]{:S(2)}) copy-start(f32[128,34,258]{0,1,2:T(8,128)S(1)} %add_convert_fusion) | copy-start | bytes 13473796
  121.1 4.8 %collective-permute-start.8 = (f32[128,1,256]{2,0,1:T(8,128)S(1)}, f32[128,1,256]{2,0,1:T(8,128)S(1)}, u32[]{:S(2)}, u32[]{:S(2)}) collective-permute-start(f32[128,1,256]{2,0,1:T(8,128)S(1)} %copy.25), channel_id=1, source_target_pairs={{4,0},{8,4},{12,8},{5,1},{9,5},{13,9},{6,2},{10,6},{14,10},{7,3},{... | collective-permute-start | bytes 393224 | tf_op jit(solution)/shard_map/ppermute | solution.py:17
  122.5 4.4 %collective-permute-start.9 = (f32[128,1,256]{2,0,1:T(8,128)S(1)}, f32[128,1,256]{2,0,1:T(8,128)S(1)}, u32[]{:S(2)}, u32[]{:S(2)}) collective-permute-start(f32[128,1,256]{2,0,1:T(8,128)S(1)} %copy.27), channel_id=1, source_target_pairs={{0,4},{4,8},{8,12},{1,5},{5,9},{9,13},{2,6},{6,10},{10,14},{3,7},{... | collective-permute-start | bytes 393224 | tf_op jit(solution)/shard_map/ppermute | solution.py:15
  127.8 17.0 %collective-permute-start.10 = (f32[128,34,1]{0,1,2:T(8,128)S(1)}, f32[128,34,1]{0,1,2:T(8,128)S(1)}, u32[]{:S(2)}, u32[]{:S(2)}) collective-permute-start(f32[128,34,1]{0,1,2:T(8,128)S(1)} %get-tuple-element.6), channel_id=1, source_target_pairs={{1,0},{2,1},{3,2},{5,4},{6,5},{7,6},{9,8},{10,9},{11,10},{13,12},{... | collective-permute-start | bytes 52232 | tf_op jit(solution)/shard_map/ppermute | solution.py:17
  129.1 15.7 %collective-permute-start.11 = (f32[128,34,1]{0,1,2:T(8,128)S(1)}, f32[128,34,1]{0,1,2:T(8,128)S(1)}, u32[]{:S(2)}, u32[]{:S(2)}) collective-permute-start(f32[128,34,1]{0,1,2:T(8,128)S(1)} %get-tuple-element.7), channel_id=1, source_target_pairs={{0,1},{1,2},{2,3},{4,5},{5,6},{6,7},{8,9},{9,10},{10,11},{12,13},{... | collective-permute-start | bytes 52232 | tf_op jit(solution)/shard_map/ppermute | solution.py:15
  133.8 11.0 %slice-start = ((s8[5283840]{0:T(1024)(128)(4,1)}), s8[1089536]{0:T(1024)(128)(4,1)S(1)}, s32[]{:S(2)}) async-start(s8[5283840]{0:T(1024)(128)(4,1)} %bitcast.24), calls=%async_computation.1 | async-start | bytes 2179072
  133.8 11.0 %copy-start.3 = (bf16[1,1,128,32,256]{2,3,4,1,0:T(8,128)(2,1)S(1)}, bf16[1,1,128,32,256]{2,3,4,1,0:T(8,128)(2,1)}, u32[]{:S(2)}) copy-start(bf16[1,1,128,32,256]{2,3,4,1,0:T(8,128)(2,1)} %copy.39) | copy-start | bytes 6291460
  139.2 5.6 %slice-start.1 = ((s8[5283840]{0:T(1024)(128)(4,1)}), s8[4194304]{0:T(1024)(128)(4,1)S(1)}, s32[]{:S(2)}) async-start(s8[5283840]{0:T(1024)(128)(4,1)} %bitcast.24), calls=%async_computation.2 | async-start | bytes 8388608
  139.2 5.6 %copy-start.1 = (f32[128,32,256]{0,1,2:T(8,128)S(1)}, f32[128,32,256]{0,1,2:T(8,128)}, u32[]{:S(2)}) copy-start(f32[128,32,256]{0,1,2:T(8,128)} %get-tuple-element.5) | copy-start | bytes 12582916
Sparse Core Ops, SparseCore 0:
  119.4 192.0 all-reduce.7
where the time goes:
time: 329 us; the launch traced here: 328 us
  waiting for transfers between devices  143 us (43%)
  local copies, waits for them, and re-layouts  81.7 us (25%)
  other arithmetic  56 us (17%)
  starting transfers between devices  32.2 us (10%)
  between operations  15 us (5%)
    psum x1, waiting for transfers between devices, shards(): summed = lax.psum(gradient, 'exp')  142 us
    unnamed x29, local copies, waits for them, and re-layouts  48.8 us
    add x1, other arithmetic, shards(): gradient = gradient + gradient_term  32.2 us
    ppermute x6, starting transfers between devices, padded(): lax.ppermute(tail, axis, [(i, (i + 1) % count) for i in range(ends)])  24.3 us
    broadcast_in_dim x1, other arithmetic, shards(): return (adjoint[None], owned)  18.8 us
    slice x2, local copies, waits for them, and re-layouts, adjoint_update(): adjoint[1:]  10.9 us
    ppermute x6, starting transfers between devices, padded(): lax.ppermute(head, axis, [((i + 1) % count, i) for i in range(ends)])  7.86 us
  transfers between devices with their start and end apart: 13, of which 2 were waited for; matrix products, arithmetic and copies ran while one was open for 28% of the time, Pallas kernels for 0%

commit v1 on v0

--- a/solution.py
+++ b/solution.py
@@ -79,7 +79,8 @@
             observed[moment, 0],
         )
         gradient = gradient + gradient_term
-    summed = lax.psum(gradient, "exp")
+    pieces = lax.all_gather(gradient, "exp", axis=0, tiled=False)
+    summed = pieces.sum(axis=0)
     owned = lax.dynamic_slice_in_dim(summed, lax.axis_index("exp") * share, share, 0)
     return (adjoint[None], owned)
 

time: 329 us -> 488 us (1.48)
  waiting for transfers between devices: 143 us -> 285 us
  other arithmetic: 56 us -> 80.5 us
  local copies, waits for them, and re-layouts: 81.7 us -> 72.1 us
    all_gather x0 -> x1, waiting for transfers between devices: none -> 284 us  [shards(): pieces = lax.all_gather(gradient, 'exp', axis=0, tiled=False)]
    psum x1 -> x0, waiting for transfers between devices: 142 us -> none  [shards(): summed = lax.psum(gradient, 'exp')]
    reduce_sum x0 -> x1, other arithmetic: none -> 14.7 us  [shards(): summed = pieces.sum(axis=0)]
    broadcast_in_dim x1, other arithmetic: 18.8 us -> 28.6 us  [shards(): return (adjoint[None], owned)]
    unnamed x29 -> x26, local copies, waits for them, and re-layouts: 48.8 us -> 41.1 us
    add x0 -> x1, local copies, waits for them, and re-layouts: none -> 5.47 us  [shards(): gradient = gradient + gradient_term]
  transfers between devices with their start and end apart: 13 -> 13, of which waited for: 2 -> 2; matrix products, arithmetic and copies ran while one was open for 28% -> 18% of each run, Pallas kernels for 0% -> 0%
where the time goes in v1:
time: 488 us; the launch traced here: 484 us
  waiting for transfers between devices  285 us (58%)
  other arithmetic  80.5 us (16%)
  local copies, waits for them, and re-layouts  72.1 us (15%)
  starting transfers between devices  32.2 us (7%)
  between operations  14.9 us (3%)
    all_gather x1, waiting for transfers between devices, shards(): pieces = lax.all_gather(gradient, 'exp', axis=0, tiled=False)  284 us
    unnamed x26, local copies, waits for them, and re-layouts  41.1 us
    add x1, other arithmetic, shards(): gradient = gradient + gradient_term  33.9 us
    broadcast_in_dim x1, other arithmetic, shards(): return (adjoint[None], owned)  28.6 us
    ppermute x6, starting transfers between devices, padded(): lax.ppermute(tail, axis, [(i, (i + 1) % count) for i in range(ends)])  24.4 us
    reduce_sum x1, other arithmetic, shards(): summed = pieces.sum(axis=0)  14.7 us
  transfers between devices with their start and end apart: 13, of which 2 were waited for; matrix products, arithmetic and copies ran while one was open for 18% of the time, Pallas kernels for 0%

profile of v1, /device:TPU:16, one launch (start us, length us, event | category | flops | bytes accessed | tf_op | source)
XLA Modules:
  0.0 484.4 jit_solution(11535588039760264501)
XLA Ops:
  7.2 5.3 %copy.9 = s32[128,32,256]{0,2,1:T(8,128)} copy(s32[128,32,256]{2,1,0:T(8,128)} %param.11) | data formatting | bytes 8388608 | tf_op args[4]
  16.5 5.4 %copy.12 = f32[1,128,32,256]{1,3,2,0:T(8,128)} copy(f32[1,128,32,256]{3,2,1,0:T(8,128)} %param.7) | data formatting | bytes 8388608 | tf_op args[0]
  24.3 5.6 %collective-permute-start.5 = (f32[128,1,256]{0,2,1:T(8,128)S(1)}, f32[128,1,256]{0,2,1:T(8,128)S(1)}, u32[]{:S(2)}, u32[]{:S(2)}) collective-permute-start(f32[128,1,256]{0,2,1:T(8,128)S(1)} %get-tuple-element.16), channel_id=1, source_target_pairs={{0,4},{4,8},{8,12},{1,5},{5,9},{9,13},{2,6},{6,10},{10,14},{3,7},{... | collective-permute-start | bytes 393224 | tf_op jit(solution)/shard_map/ppermute | solution.py:15
  29.9 5.3 %slice_bitcast_fusion = f32[127,32,256]{0,2,1:T(8,128)} fusion(f32[1,128,32,256]{1,3,2,0:T(8,128)} %copy.12), kind=kLoop, calls=%fused_computation.72 | loop fusion | bytes 8323072 | tf_op jit(solution)/shard_map/slice | solution.py:45
  35.2 2.6 fusion.65
  38.9 2.5 fusion.62
  42.7 3.4 copy.23
  46.2 4.6 copy.21
  50.7 4.5 copy.22
  55.2 5.3 %copy.14 = f32[128,32,256]{0,2,1:T(8,128)} copy(f32[128,32,256]{2,1,0:T(8,128)} %param.10) | data formatting | bytes 8388608 | tf_op args[3]
  61.7 3.7 collective-permute-start.2
  68.1 5.2 %collective-permute-start.7 = (f32[128,34,1]{0,2,1:T(1,128)S(1)}, f32[128,34,1]{0,2,1:T(1,128)S(1)}, u32[]{:S(2)}, u32[]{:S(2)}) collective-permute-start(f32[128,34,1]{0,2,1:T(1,128)S(1)} %get-tuple-element.9), channel_id=1, source_target_pairs={{0,1},{1,2},{2,3},{4,5},{5,6},{6,7},{8,9},{9,10},{10,11},{12,13},{... | collective-permute-start | bytes 52232 | tf_op jit(solution)/shard_map/ppermute | solution.py:15
  73.8 2.8 slice.175
  76.6 3.2 slice.182
  79.8 33.9 %fusion.9 = (f32[128,32,256]{0,2,1:T(8,128)}, f32[128,32,256]{0,2,1:T(8,128)}) fusion(bf16[1,1,128,32,256]{2,4,3,1,0:T(8,128)(2,1)S(1)} %copy.23, bf16[1,1,128,32,256]{2,4,3,1,0:T(8,128)(2,1)} %copy.21, f32[]{:T(128)} %fusion.60, f32[1,128,32,256]{1,3,2,0:T(8,128)} %copy.12, f32[128,34,258]{0,2,1:T(8,128)S(1)} %add_convert_fusion, ...), kind=kLoop, calls=%fused_computation.22 | loop fusion | flops 57671680 | bytes 61048836 | tf_op jit(solution)/shard_map/add | solution.py:81
  113.7 5.5 %copy.19 = f32[128,32,256]{2,1,0:T(8,128)} copy(f32[128,32,256]{0,2,1:T(8,128)} %get-tuple-element.4) | data formatting | bytes 8388608 | tf_op jit(solution)/shard_map/add | solution.py:81
  121.5 3.4 collective-permute-start.9
  128.2 4.7 collective-permute-start.11
  132.9 4.7 copy.24
  137.7 4.3 slice.186
  143.3 28.6 %fusion.59 = f32[1,128,32,256]{1,3,2,0:T(8,128)} fusion(f32[128,32,256]{0,2,1:T(8,128)} %slice.175, f32[128,32,256]{0,2,1:T(8,128)} %get-tuple-element.5, f32[127,32,256]{0,2,1:T(8,128)S(1)} %slice.186, f32[128,1,256]{0,2,1:T(8,128)S(1)} %collective-permute-done.8, f32[128,1,256]{0,2,1:T(8,128)S(1)} %collective-permute-done.9, ...), kind=kLoop, calls=%fused_computation.89 | loop fusion | flops 45088768 | bytes 46368772 | tf_op jit(solution)/shard_map/broadcast_in_dim | solution.py:85
  171.8 5.4 %copy.20 = f32[1,128,32,256]{3,2,1,0:T(8,128)} copy(f32[1,128,32,256]{1,3,2,0:T(8,128)} %fusion.59) | data formatting | bytes 8388608
  177.3 283.6 %all-gather.3.cloned.1.call-done = f32[1024,32,256]{2,1,0:T(8,128)} async-done(((f32[128,32,256]{2,1,0:T(8,128)}), f32[1024,32,256]{2,1,0:T(8,128)}) %all-gather.3.cloned.1.call-update) | async-done | bytes 33554448 | tf_op jit(solution)/shard_map/all_gather | solution.py:82
  460.9 14.7 %reduce_sum.19 = f32[128,32,256]{2,1,0:T(8,128)} reduce(f32[8,128,32,256]{3,2,1,0:T(8,128)} %bitcast.30, f32[]{:T(128)} %constant.9.clone.1), dimensions={0}, to_apply=%region_1.2 | reduce | flops 7340032 | bytes 37748740 | tf_op jit(solution)/shard_map/reduce_sum | solution.py:83
  (49 shorter events, 21.1 us)
Async XLA Ops:
  7.2 453.7 %all-gather.3.cloned.1.call-start = ((), (), s32[]{:S(2)}) async-start(), calls=%async_computation | async-start | bytes 37748736 | tf_op jit(solution)/shard_map/all_gather | solution.py:82
  13.5 47.1 %collective-permute-start = (s32[128,1,256]{0,2,1:T(8,128)S(1)}, s32[128,1,256]{0,2,1:T(8,128)S(1)}, u32[]{:S(2)}, u32[]{:S(2)}) collective-permute-start(s32[128,1,256]{0,2,1:T(8,128)S(1)} %get-tuple-element.20), channel_id=1, source_target_pairs={{0,4},{4,8},{8,12},{1,5},{5,9},{9,13},{2,6},{6,10},{10,14},{3,7},{... | collective-permute-start | bytes 393224 | tf_op jit(solution)/shard_map/ppermute | solution.py:15
  15.2 45.3 %collective-permute-start.1 = (s32[128,1,256]{0,2,1:T(8,128)S(1)}, s32[128,1,256]{0,2,1:T(8,128)S(1)}, u32[]{:S(2)}, u32[]{:S(2)}) collective-permute-start(s32[128,1,256]{0,2,1:T(8,128)S(1)} %get-tuple-element.21), channel_id=1, source_target_pairs={{4,0},{8,4},{12,8},{5,1},{9,5},{13,9},{6,2},{10,6},{14,10},{7,3},{... | collective-permute-start | bytes 393224 | tf_op jit(solution)/shard_map/ppermute | solution.py:17
  22.9 43.7 %collective-permute-start.4 = (f32[128,1,256]{0,2,1:T(8,128)S(1)}, f32[128,1,256]{0,2,1:T(8,128)S(1)}, u32[]{:S(2)}, u32[]{:S(2)}) collective-permute-start(f32[128,1,256]{0,2,1:T(8,128)S(1)} %get-tuple-element.17), channel_id=1, source_target_pairs={{4,0},{8,4},{12,8},{5,1},{9,5},{13,9},{6,2},{10,6},{14,10},{7,3},{... | collective-permute-start | bytes 393224 | tf_op jit(solution)/shard_map/ppermute | solution.py:17
  24.2 10.9 %copy-start.4 = (bf16[2,1,128,32,256]{4,3,2,1,0:T(8,128)(2,1)S(1)}, bf16[2,1,128,32,256]{4,3,2,1,0:T(8,128)(2,1)}, u32[]{:S(2)}) copy-start(bf16[2,1,128,32,256]{4,3,2,1,0:T(8,128)(2,1)} %param.8) | copy-start | bytes 12582916
  24.3 42.4 %collective-permute-start.5 = (f32[128,1,256]{0,2,1:T(8,128)S(1)}, f32[128,1,256]{0,2,1:T(8,128)S(1)}, u32[]{:S(2)}, u32[]{:S(2)}) collective-permute-start(f32[128,1,256]{0,2,1:T(8,128)S(1)} %get-tuple-element.16), channel_id=1, source_target_pairs={{0,4},{4,8},{8,12},{1,5},{5,9},{9,13},{2,6},{6,10},{10,14},{3,7},{... | collective-permute-start | bytes 393224 | tf_op jit(solution)/shard_map/ppermute | solution.py:15
  35.2 3.7 copy-start.5
  38.9 3.1 copy-start.6
  60.6 6.2 %copy-start.1 = (f32[1,128,32,256]{1,3,2,0:T(8,128)S(1)}, f32[1,128,32,256]{1,3,2,0:T(8,128)}, u32[]{:S(2)}) copy-start(f32[1,128,32,256]{1,3,2,0:T(8,128)} %copy.12) | copy-start | bytes 12582916
  60.6 12.7 %copy-start.2 = (s32[128,32,256]{0,2,1:T(8,128)S(1)}, s32[128,32,256]{0,2,1:T(8,128)}, u32[]{:S(2)}) copy-start(s32[128,32,256]{0,2,1:T(8,128)} %copy.9) | copy-start | bytes 12582916
  61.7 11.5 %collective-permute-start.2 = (s32[128,34,1]{0,2,1:T(1,128)S(1)}, s32[128,34,1]{0,2,1:T(1,128)S(1)}, u32[]{:S(2)}, u32[]{:S(2)}) collective-permute-start(s32[128,34,1]{0,2,1:T(1,128)S(1)} %get-tuple-element.10), channel_id=1, source_target_pairs={{0,1},{1,2},{2,3},{4,5},{5,6},{6,7},{8,9},{9,10},{10,11},{12,13},{... | collective-permute-start | bytes 52232 | tf_op jit(solution)/shard_map/ppermute | solution.py:15
  65.4 7.9 %collective-permute-start.3 = (s32[128,34,1]{0,2,1:T(1,128)S(1)}, s32[128,34,1]{0,2,1:T(1,128)S(1)}, u32[]{:S(2)}, u32[]{:S(2)}) collective-permute-start(s32[128,34,1]{0,2,1:T(1,128)S(1)} %get-tuple-element.11), channel_id=1, source_target_pairs={{1,0},{2,1},{3,2},{5,4},{6,5},{7,6},{9,8},{10,9},{11,10},{13,12},{... | collective-permute-start | bytes 52232 | tf_op jit(solution)/shard_map/ppermute | solution.py:17
  66.8 13.0 %collective-permute-start.6 = (f32[128,34,1]{0,2,1:T(1,128)S(1)}, f32[128,34,1]{0,2,1:T(1,128)S(1)}, u32[]{:S(2)}, u32[]{:S(2)}) collective-permute-start(f32[128,34,1]{0,2,1:T(1,128)S(1)} %get-tuple-element.8), channel_id=1, source_target_pairs={{1,0},{2,1},{3,2},{5,4},{6,5},{7,6},{9,8},{10,9},{11,10},{13,12},{... | collective-permute-start | bytes 52232 | tf_op jit(solution)/shard_map/ppermute | solution.py:17
  68.1 11.7 %collective-permute-start.7 = (f32[128,34,1]{0,2,1:T(1,128)S(1)}, f32[128,34,1]{0,2,1:T(1,128)S(1)}, u32[]{:S(2)}, u32[]{:S(2)}) collective-permute-start(f32[128,34,1]{0,2,1:T(1,128)S(1)} %get-tuple-element.9), channel_id=1, source_target_pairs={{0,1},{1,2},{2,3},{4,5},{5,6},{6,7},{8,9},{9,10},{10,11},{12,13},{... | collective-permute-start | bytes 52232 | tf_op jit(solution)/shard_map/ppermute | solution.py:15
  73.8 6.0 %copy-start = (f32[128,34,258]{0,2,1:T(8,128)}, f32[128,34,258]{0,2,1:T(8,128)S(1)}, u32[]{:S(2)}) copy-start(f32[128,34,258]{0,2,1:T(8,128)S(1)} %add_convert_fusion) | copy-start | bytes 13473796
  120.2 4.7 collective-permute-start.8
  121.5 4.4 collective-permute-start.9
  126.9 15.1 %collective-permute-start.10 = (f32[128,34,1]{0,2,1:T(1,128)S(1)}, f32[128,34,1]{0,2,1:T(1,128)S(1)}, u32[]{:S(2)}, u32[]{:S(2)}) collective-permute-start(f32[128,34,1]{0,2,1:T(1,128)S(1)} %get-tuple-element.6), channel_id=1, source_target_pairs={{1,0},{2,1},{3,2},{5,4},{6,5},{7,6},{9,8},{10,9},{11,10},{13,12},{... | collective-permute-start | bytes 52232 | tf_op jit(solution)/shard_map/ppermute | solution.py:17
  128.2 13.8 %collective-permute-start.11 = (f32[128,34,1]{0,2,1:T(1,128)S(1)}, f32[128,34,1]{0,2,1:T(1,128)S(1)}, u32[]{:S(2)}, u32[]{:S(2)}) collective-permute-start(f32[128,34,1]{0,2,1:T(1,128)S(1)} %get-tuple-element.7), channel_id=1, source_target_pairs={{0,1},{1,2},{2,3},{4,5},{5,6},{6,7},{8,9},{9,10},{10,11},{12,13},{... | collective-permute-start | bytes 52232 | tf_op jit(solution)/shard_map/ppermute | solution.py:15
  137.7 4.3 slice-start
  137.7 4.9 %slice-start.1 = ((s8[4595712]{0:T(1024)(128)(4,1)}), s8[4194304]{0:T(1024)(128)(4,1)S(1)}, s32[]{:S(2)}) async-start(s8[4595712]{0:T(1024)(128)(4,1)} %bitcast.25), calls=%async_computation.2 | async-start | bytes 8388608
  137.7 5.6 %copy-start.3 = (bf16[1,1,128,32,256]{2,4,3,1,0:T(8,128)(2,1)S(1)}, bf16[1,1,128,32,256]{2,4,3,1,0:T(8,128)(2,1)}, u32[]{:S(2)}) copy-start(bf16[1,1,128,32,256]{2,4,3,1,0:T(8,128)(2,1)} %copy.24) | copy-start | bytes 6291460
Sparse Core Ops, SparseCore 0:
  119.3 341.5 all-gather.2
